TPU v7x, 32 devices: a whole 2x2x4 slice. The times are simulated.
32 devices in a mesh: groups: 2 (over y), zone: 4 (over z), scen: 2 (over x), hour: 2 (over core).
Axes of the slice: x: 2, y: 2, z: 4, core: 2. Of those that a mesh axis runs over, the one named last changes fastest.
Arguments:
- forcing: bfloat16 [1024, 48, 64], P(('groups', 'zone', 'scen', 'hour')), parts along dimension 0, may hold values from -3 to 3
- response: bfloat16 [48, 64, 8192], P('hour', None, ('groups', 'zone')), parts along dimension 2, may hold values from -0.75 to 0.75
- window_params: float32 [128, 64], P('groups'), parts along dimension 0, may hold values from 0.5 to 1.5
- building_map: int32 [8192], P(('groups', 'zone')), parts along dimension 0, may hold values from 0 to 1023
- owner_ids: int32 [2048], P('groups'), parts along dimension 0, may hold values from 0 to 63
- band_ids: int32 [48, 8192], P('hour', ('groups', 'zone')), parts along dimension 1, may hold values from 0 to 7
- floor_area: float32 [8192], P(('groups', 'zone')), parts along dimension 0, may hold values from 0.5 to 18, as said below
Outputs:
- sensitivity: float32 [128, 64], P(('groups', 'zone', 'scen', 'hour')), parts along dimension 0
- objective: float32 [2], P('groups'), parts along dimension 0
There are 2 independent parts, one for each index of `groups`. A program takes and returns all parts, laid end to end along the dimension named above; each array names one. Nothing has to cross between parts.
Inputs may be any that keep to these rules, and one draw needn't show every extreme that they name: `floor_area`: floor areas are positive.
All inputs are finite; a program needn't handle non-finite values.
Results may differ from a plain program's by a relative error of at most 0.0006.
Values may be sent and summed in bfloat16 or wider, within the bound.
A program may use at most 128 MiB of HBM per device.

v0:
```python
import math
import jax
import jax.numpy as jnp
from jax import lax
from jax.sharding import PartitionSpec as P

SHARPNESS = 200.0


def joined(value, axis, join):
    pieces = jax.tree.map(lambda part: lax.all_gather(part, axis), value)
    head = jax.tree.map(lambda part: part[0], pieces)
    tail = jax.tree.map(lambda part: part[1:], pieces)
    running, _ = lax.scan(lambda running, share: (join(running, share), None), head, tail)
    return running


def merge_softmax(first, second):
    highest = jnp.maximum(first[0], second[0])
    return (
        highest,
        first[1] * jnp.exp(first[0] - highest) + second[1] * jnp.exp(second[0] - highest),
    )


def on_device(forcing, response, window_params, building_map, owner_ids, band_ids, floor_area):
    hour_local = response.shape[0]
    width = response.shape[1]
    zone_local = response.shape[2]
    hours_total = hour_local * lax.axis_size("hour")
    hour_first = lax.axis_index("hour") * hour_local
    positions = (hour_first + jnp.arange(hour_local)).astype(jnp.float32)
    occupant_level = 1.0 + 2.0 * positions / (hours_total - 1)
    candidate_plan = jnp.take(owner_ids, building_map)
    zone_parameters = jnp.take(window_params, candidate_plan, axis=0)
    coeff = (response.astype(jnp.float32) * zone_parameters.T[None, :, :]).astype(jnp.bfloat16)
    band_low = 0.25 * (band_ids.astype(jnp.float32) - 3.5) - 0.5
    band_high = band_low + 1.0
    zone_weight = occupant_level[:, None] * floor_area[None, :]
    block_count = hour_local // 8
    mine = lax.all_to_all(forcing, "hour", split_axis=1, concat_axis=0, tiled=True)

    def inside_climate_state(outlook_records, initial_clock_time):
        record_elements = lax.slice_in_dim(
            outlook_records, initial_clock_time, initial_clock_time + 8, axis=1
        )
        thermal_demand = jnp.einsum(
            "shp,hpz->hsz",
            record_elements,
            coeff[initial_clock_time : initial_clock_time + 8],
            preferred_element_type=jnp.float32,
        )
        return (thermal_demand, record_elements)

    weight_part = (jnp.sum(floor_area) * jnp.sum(occupant_level)).reshape(1)
    outlook_records = lax.all_gather(mine, "zone", axis=0, tiled=True)
    sums = jnp.zeros((outlook_records.shape[0],), jnp.float32)
    for hour_block in range(block_count):
        initial_clock_time = hour_block * 8
        thermal_demand, record_elements = inside_climate_state(outlook_records, initial_clock_time)
        low = band_low[initial_clock_time : initial_clock_time + 8][:, None, :]
        high = band_high[initial_clock_time : initial_clock_time + 8][:, None, :]
        penalty = jax.nn.softplus(thermal_demand - high) + jax.nn.softplus(low - thermal_demand)
        sums = sums + jnp.sum(
            penalty * zone_weight[initial_clock_time : initial_clock_time + 8][:, None, :],
            axis=(0, 2),
        )
    loss_sum, weight_total = lax.psum((sums, weight_part), ("zone", "hour"))
    scores = SHARPNESS * loss_sum / weight_total[0]
    local_peak = jnp.max(scores)
    peak_score, exp_total = joined(
        (local_peak, jnp.sum(jnp.exp(scores - local_peak))), "scen", merge_softmax
    )
    objective = ((peak_score + jnp.log(exp_total)) / SHARPNESS).reshape(1)
    scen_weight = jnp.exp(scores - peak_score) / exp_total / weight_total[0]
    empty = jnp.zeros((width, zone_local), jnp.float32)
    accumulated = empty
    outlook_records = lax.all_gather(mine, "zone", axis=0, tiled=True)
    for hour_block in range(block_count):
        initial_clock_time = hour_block * 8
        thermal_demand, record_elements = inside_climate_state(outlook_records, initial_clock_time)
        low = band_low[initial_clock_time : initial_clock_time + 8][:, None, :]
        high = band_high[initial_clock_time : initial_clock_time + 8][:, None, :]
        slope = jax.nn.sigmoid(thermal_demand - high) - jax.nn.sigmoid(low - thermal_demand)
        adjoint = (
            slope
            * scen_weight[None, :, None]
            * zone_weight[initial_clock_time : initial_clock_time + 8][:, None, :]
        ).astype(jnp.bfloat16)
        mixed = jnp.einsum(
            "shp,hsz->hpz", record_elements, adjoint, preferred_element_type=jnp.float32
        )
        accumulated = accumulated + jnp.sum(
            response[initial_clock_time : initial_clock_time + 8].astype(jnp.float32) * mixed,
            axis=0,
        )
    zones_all = zone_local * lax.axis_size("zone")
    designs = window_params.shape[0]
    gain = math.sqrt(width * zones_all * hours_total * designs)
    zone_rows = accumulated.T
    owners_local = designs // (
        lax.axis_size("zone") * lax.axis_size("scen") * lax.axis_size("hour")
    )
    onehot = (
        candidate_plan[:, None]
        == jnp.arange(owners_local * lax.axis_size(("zone", "scen", "hour")))[None, :]
    ).astype(jnp.float32)
    sensitivity = lax.psum_scatter(
        gain * jnp.dot(onehot.T, zone_rows, precision=lax.Precision.HIGHEST),
        ("zone", "scen", "hour"),
        scatter_dimension=0,
        tiled=True,
    )
    return (sensitivity, objective)


def solution(mesh):
    in_specs = (
        P(("groups", "zone", "scen", "hour"), None, None),
        P("hour", None, ("groups", "zone")),
        P("groups", None),
        P(("groups", "zone")),
        P("groups"),
        P("hour", ("groups", "zone")),
        P(("groups", "zone")),
    )
    out_specs = (P(("groups", "zone", "scen", "hour"), None), P("groups"))
    return jax.shard_map(
        on_device, mesh=mesh, in_specs=in_specs, out_specs=out_specs, check_vma=False
    )
```

profile of v0, /device:TPU:0, one launch (start us, length us, event | category | flops | bytes accessed | tf_op | source)
XLA Modules:
  0.0 207.4 jit_solution(13071616913442641954)
XLA Ops:
  0.7 1.2 copy.37
  1.8 1.0 reshape.77
  2.9 3.4 %all-to-all-start = ((bf16[2,2,24576]{2,1,0:T(2,128)(2,1)}), bf16[2,2,24576]{2,1,0:T(2,128)(2,1)S(1)}, u32[]{:S(2)}, u32[]{:S(2)}) async-start(bf16[2,2,24576]{2,1,0:T(2,128)(2,1)} %reshape.77), calls=%async_computation | async-start | bytes 393216 | tf_op jit(solution)/shard_map/all_to_all | solution.py:41
  6.3 1.5 all-to-all-done
  7.8 0.3 reshape.78
  8.2 31.7 %all_gather.16 = bf16[256,24,64]{2,1,0:T(8,128)(2,1)S(1)} all-gather(bf16[64,24,64]{2,1,0:T(8,128)(2,1)S(1)} %bitcast.231), channel_id=1, replica_groups=mesh['groups'=2,'zone'=4,'scen'=2,'hour'=2] {'zone'}, dimensions={0}, use_global_device_ids=true | all-gather | bytes 983040 | tf_op jit(solution)/shard_map/all_gather | solution.py:78
  40.2 0.3 copy.35
  40.6 0.6 multiply_add_fusion
  41.3 4.5 %gather_fusion = s32[1024]{0:T(1024)S(1)} fusion(s32[1024]{0:T(1024)S(1)} %copy-done.1, s32[1024]{0:T(1024)S(1)} %fusion.88), kind=kCustom, calls=%fused_computation | custom fusion | bytes 12288 | tf_op jit(solution)/shard_map/jit(_take)/gather | solution.py:34
  45.9 2.8 %gather_fusion.1 = f32[1024,64]{1,0:T(8,128)S(1)} fusion(f32[64,64]{1,0:T(8,128)S(1)} %copy-done, s32[1024]{0:T(1024)S(1)} %fusion.89), kind=kCustom, calls=%fused_computation.1 | custom fusion | bytes 528384 | tf_op jit(solution)/shard_map/jit(_take)/gather | solution.py:35
  49.1 0.3 copy.33
  49.5 0.3 copy.34
  49.8 0.6 reduce_sum.84
  51.7 13.8 %fusion.8 = (f32[256]{0:T(256)S(1)}, f32[8,1024,256]{2,1,0:T(8,128)}) fusion(f32[8,1024]{1,0:T(8,128)S(1)} %get-tuple-element.35, f32[8,1024]{1,0:T(8,128)S(1)} %get-tuple-element.52, f32[8,1024]{1,0:T(8,128)S(1)} %get-tuple-element.29, bf16[256,8,64]{0,2,1:T(8,128)(2,1)S(1)} %copy.35, bf16[24,64,1024]{2,1,0:T(8,128)(2,1)} %param.8, f32[64,1024]{1,0:T(8,128)S(1)} %copy.19), kind=kOutput, calls=%fused_computation.16 | convolution fusion | flops 308805376 | bytes 12157952 | tf_op jit(solution)/shard_map/shp,hpz->hsz/dot_general | solution.py:47
  65.5 13.3 %fusion.2 = (f32[256]{0:T(256)S(1)}, f32[8,1024,256]{2,1,0:T(8,128)}) fusion(f32[8,1024]{1,0:T(8,128)S(1)} %get-tuple-element.36, f32[8,1024]{1,0:T(8,128)S(1)} %get-tuple-element.51, f32[8,1024]{1,0:T(8,128)S(1)} %get-tuple-element.30, bf16[256,8,64]{0,2,1:T(8,128)(2,1)S(1)} %copy.33, bf16[24,64,1024]{2,1,0:T(8,128)(2,1)S(1)} %copy-done.5, ...), kind=kOutput, calls=%fused_computation.10 | convolution fusion | flops 308805376 | bytes 12157952 | tf_op jit(solution)/shard_map/shp,hpz->hsz/dot_general | solution.py:47
  78.8 13.2 %fusion.5 = (f32[256]{0:T(256)S(1)}, f32[8,1024,256]{2,1,0:T(8,128)}) fusion(f32[8,1024]{1,0:T(8,128)S(1)} %get-tuple-element.34, f32[8,1024]{1,0:T(8,128)S(1)} %get-tuple-element.53, f32[8,1024]{1,0:T(8,128)S(1)} %get-tuple-element.28, bf16[256,8,64]{0,2,1:T(8,128)(2,1)S(1)} %copy.34, bf16[24,64,1024]{2,1,0:T(8,128)(2,1)S(1)} %copy-done.5, ...), kind=kOutput, calls=%fused_computation.13 | convolution fusion | flops 308805376 | bytes 12157952 | tf_op jit(solution)/shard_map/shp,hpz->hsz/dot_general | solution.py:47
  92.0 16.5 %all-reduce.3 = (f32[256]{0:T(256)S(1)}, f32[]{:T(128)}) all-reduce(f32[256]{0:T(256)S(1)} %add_add_fusion, f32[]{:T(128)S(6)} %mul.142), channel_id=1, replica_groups=mesh['groups'=2,'zone'=4,'scen'=2,'hour'=2] {'zone','hour'}, use_global_device_ids=true, to_apply=%region_3.4 | all-reduce | flops 257 | bytes 2056 | tf_op jit(solution)/shard_map/psum | solution.py:68
  108.5 1.2 fusion.94
  109.8 1.3 exponential_reduce_fusion
  111.0 0.6 dynamic-slice
  111.6 1.3 dynamic-update-slice.1
  112.9 1.3 dynamic-update-slice
  114.2 5.1 %all-reduce.4 = (f32[2]{0:T(128)S(1)}, f32[2]{0:T(128)S(1)}) all-reduce(f32[2]{0:T(128)S(1)} %dynamic-update-slice.1, f32[2]{0:T(128)S(1)} %dynamic-update-slice), channel_id=1, replica_groups=mesh['groups'=2,'zone'=4,'scen'=2,'hour'=2] {'scen'}, use_global_device_ids=true, to_apply=%add.1 | all-reduce | flops 4 | bytes 32
  119.3 0.6 fusion.100
  122.5 0.6 fusion.99
  125.1 8.3 %fusion.72 = f32[64,1024]{1,0:T(8,128)S(1)} fusion(bf16[256,8,64]{0,2,1:T(8,128)(2,1)S(1)} %copy.35, f32[8,1024,256]{2,1,0:T(8,128)} %get-tuple-element.44, f32[256]{0:T(256)S(1)} %exponential_divide_fusion, f32[8,1024]{1,0:T(8,128)S(1)} %get-tuple-element.35, f32[8,1024]{1,0:T(8,128)S(1)} %get-tuple-element.52, f32[8,1024]{1,0:T(8,128)S(1)} %get-tuple-element.29, ...), kind=kOutput, calls=%fused_computation.97 | convolution fusion | flops 295108608 | bytes 10060800 | tf_op jit(solution)/shard_map/shp,hsz->hpz/dot_general | solution.py:90
  133.5 6.3 %fusion.74 = f32[64,1024]{1,0:T(8,128)S(1)} fusion(bf16[256,8,64]{0,2,1:T(8,128)(2,1)S(1)} %copy.33, f32[8,1024,256]{2,1,0:T(8,128)S(1)} %copy-done.9, f32[256]{0:T(256)S(1)} %exponential_divide_fusion, f32[8,1024]{1,0:T(8,128)S(1)} %get-tuple-element.36, f32[8,1024]{1,0:T(8,128)S(1)} %get-tuple-element.51, f32[8,1024]{1,0:T(8,128)S(1)} %get-tuple-element.30, ...), kind=kOutput, calls=%fused_computation.101 | convolution fusion | flops 295108608 | bytes 10060800 | tf_op jit(solution)/shard_map/shp,hsz->hpz/dot_general | solution.py:90
  139.9 6.3 %fusion.73 = f32[64,1024]{1,0:T(8,128)S(1)} fusion(bf16[256,8,64]{0,2,1:T(8,128)(2,1)S(1)} %copy.34, f32[8,1024,256]{2,1,0:T(8,128)S(1)} %bitcast.233, f32[256]{0:T(256)S(1)} %exponential_divide_fusion, f32[8,1024]{1,0:T(8,128)S(1)} %get-tuple-element.34, f32[8,1024]{1,0:T(8,128)S(1)} %get-tuple-element.53, f32[8,1024]{1,0:T(8,128)S(1)} %get-tuple-element.28, ...), kind=kOutput, calls=%fused_computation.99 | convolution fusion | flops 295108608 | bytes 10060800 | tf_op jit(solution)/shard_map/shp,hsz->hpz/dot_general | solution.py:90
  146.2 0.6 convolution_multiply_fusion
  146.8 57.6 %all-reduce.2 = f32[64,64]{1,0:T(8,128)S(1)} all-reduce(f32[64,64]{1,0:T(8,128)S(1)} %convolution_multiply_fusion), channel_id=2, replica_groups=mesh['groups'=2,'zone'=4,'scen'=2,'hour'=2] {'zone','scen','hour'}, use_global_device_ids=true, to_apply=%region_12.13.clone | all-reduce | flops 4096 | bytes 32768
  204.4 0.6 dynamic-slice.2
  205.7 0.6 constant_dynamic-slice_fusion
  (40 shorter events, 1.0 us)
Async XLA Ops:
  0.6 45.3 %copy-start = (f32[64,64]{1,0:T(8,128)S(1)}, f32[64,64]{1,0:T(8,128)}, u32[]{:S(2)}) copy-start(f32[64,64]{1,0:T(8,128)} %param.9) | copy-start | bytes 49156
  0.6 40.5 %copy-start.3 = (f32[1024]{0:T(1024)S(1)}, f32[1024]{0:T(1024)}, u32[]{:S(2)}) copy-start(f32[1024]{0:T(1024)} %param.13) | copy-start | bytes 12292
  0.7 40.6 %copy-start.2 = (s32[24,1024]{1,0:T(8,128)S(1)}, s32[24,1024]{1,0:T(8,128)}, u32[]{:S(2)}) copy-start(s32[24,1024]{1,0:T(8,128)} %param.12) | copy-start | bytes 294916
  0.7 40.6 %copy-start.4 = (s32[1024]{0:T(1024)S(1)}, s32[1024]{0:T(1024)}, u32[]{:S(2)}) copy-start(s32[1024]{0:T(1024)} %param.10) | copy-start | bytes 12292
  0.7 40.7 %copy-start.1 = (s32[1024]{0:T(1024)S(1)}, s32[1024]{0:T(1024)}, u32[]{:S(2)}) copy-start(s32[1024]{0:T(1024)} %param.11) | copy-start | bytes 12292
  2.9 4.9 %all-to-all-start = ((bf16[2,2,24576]{2,1,0:T(2,128)(2,1)}), bf16[2,2,24576]{2,1,0:T(2,128)(2,1)S(1)}, u32[]{:S(2)}, u32[]{:S(2)}) async-start(bf16[2,2,24576]{2,1,0:T(2,128)(2,1)} %reshape.77), calls=%async_computation | async-start | bytes 393216 | tf_op jit(solution)/shard_map/all_to_all | solution.py:41
  51.7 13.8 %copy-start.5 = (bf16[24,64,1024]{2,1,0:T(8,128)(2,1)S(1)}, bf16[24,64,1024]{2,1,0:T(8,128)(2,1)}, u32[]{:S(2)}) copy-start(bf16[24,64,1024]{2,1,0:T(8,128)(2,1)} %param.8) | copy-start | bytes 9437188
  78.8 32.3 %copy-start.8 = (u32[32]{0:T(128)S(1)}, u32[32]{0:T(128)}, u32[]{:S(2)}) copy-start(u32[32]{0:T(128)} %constant.81) | copy-start | bytes 388
  125.1 8.4 %copy-start.6 = (bf16[24,64,1024]{2,1,0:T(8,128)(2,1)S(1)}, bf16[24,64,1024]{2,1,0:T(8,128)(2,1)}, u32[]{:S(2)}) copy-start(bf16[24,64,1024]{2,1,0:T(8,128)(2,1)} %param.8) | copy-start | bytes 9437188
  125.1 8.3 %copy-start.9 = (f32[8,1024,256]{2,1,0:T(8,128)S(1)}, f32[8,1024,256]{2,1,0:T(8,128)}, u32[]{:S(2)}) copy-start(f32[8,1024,256]{2,1,0:T(8,128)} %get-tuple-element.46) | copy-start | bytes 25165828
  125.1 14.7 %slice-start = ((s8[8388608]{0:T(1024)(128)(4,1)}), s8[4194304]{0:T(1024)(128)(4,1)S(1)}, s32[]{:S(2)}) async-start(s8[8388608]{0:T(1024)(128)(4,1)} %bitcast.232), calls=%async_computation.1 | async-start | bytes 8388608
  133.5 6.4 %slice-start.1 = ((s8[8388608]{0:T(1024)(128)(4,1)}), s8[4194304]{0:T(1024)(128)(4,1)S(1)}, s32[]{:S(2)}) async-start(s8[8388608]{0:T(1024)(128)(4,1)} %bitcast.232), calls=%async_computation.2 | async-start | bytes 8388608
  139.9 64.6 %copy-start.7 = (u32[32]{0:T(128)S(1)}, u32[32]{0:T(128)}, u32[]{:S(2)}) copy-start(u32[32]{0:T(128)} %constant.93) | copy-start | bytes 388
where the time goes:
time: 208 us; the launch traced here: 207 us
  blocking collectives  111 us (53%)
  matrix products  61.8 us (30%)
  local copies, waits for them, and re-layouts  17 us (8%)
  between operations  8.65 us (4%)
  other arithmetic  4.05 us (2%)
  starting transfers between devices  3.43 us (2%)
    unnamed x2, blocking collectives  62.7 us
    dot_general x3, matrix products, inside_climate_state(): jnp.einsum('shp,hpz->hsz', record_elements, coeff[initial_clock_time:init...  40.3 us
    all_gather x1, blocking collectives, on_device(): outlook_records = lax.all_gather(mine, 'zone', axis=0, tiled=True)  31.7 us
    dot_general x3, matrix products, on_device(): jnp.einsum('shp,hsz->hpz', record_elements, adjoint, preferred_element_ty...  20.9 us
    psum x1, blocking collectives, on_device(): loss_sum, weight_total = lax.psum((sums, weight_part), ('zone', 'hour'))  16.5 us
    unnamed x37, local copies, waits for them, and re-layouts  7.84 us
    gather x1, local copies, waits for them, and re-layouts, on_device(): candidate_plan = jnp.take(owner_ids, building_map)  4.53 us
  transfers between devices with their start and end apart: 1, of which 1 were waited for; matrix products, arithmetic and copies ran while one was open for 0% of the time, Pallas kernels for 0%

commit v1 on v0

--- a/solution.py
+++ b/solution.py
@@ -38,7 +38,10 @@
     band_high = band_low + 1.0
     zone_weight = occupant_level[:, None] * floor_area[None, :]
     block_count = hour_local // 8
-    mine = lax.all_to_all(forcing, "hour", split_axis=1, concat_axis=0, tiled=True)
+    mine = jnp.concatenate(
+        lax.all_to_all(jnp.stack(jnp.split(forcing, lax.axis_size("hour"), axis=1)), "hour", 0, 0),
+        axis=0,
+    )
 
     def inside_climate_state(outlook_records, initial_clock_time):
         record_elements = lax.slice_in_dim(

time: 208 us -> 233 us (1.12)
  other arithmetic: 4.05 us -> 43.3 us
  matrix products: 61.8 us -> 34.8 us
  local copies, waits for them, and re-layouts: 17 us -> 29.4 us
    reduce_sum x0 -> x3, other arithmetic: none -> 33 us  [on_device(): jnp.sum(penalty * zone_weight[initial_clock_time:initial_clock_time + 8][...]
    dot_general x3, matrix products: 40.3 us -> 13.7 us  [inside_climate_state(): jnp.einsum('shp,hpz->hsz', record_elements, coeff[initial_clock_time:init...]
    unnamed x37 -> x78, local copies, waits for them, and re-layouts: 7.84 us -> 14 us
    convert_element_type x0 -> x1, other arithmetic: none -> 2.69 us  [on_device(): (response.astype(jnp.float32) * zone_parameters.T[None, :, :]).astype(jnp...]
  transfers between devices with their start and end apart: 1 -> 1, of which waited for: 1 -> 0; matrix products, arithmetic and copies ran while one was open for 0% -> 1% of each run, Pallas kernels for 0% -> 0%
where the time goes in v1:
time: 233 us; the launch traced here: 232 us
  blocking collectives  112 us (48%)
  other arithmetic  43.3 us (19%)
  matrix products  34.8 us (15%)
  local copies, waits for them, and re-layouts  29.4 us (13%)
  between operations  9 us (4%)
  starting transfers between devices  3.43 us (1%)
    unnamed x2, blocking collectives  62.7 us
    reduce_sum x3, other arithmetic, on_device(): jnp.sum(penalty * zone_weight[initial_clock_time:initial_clock_time + 8][...  33 us
    all_gather x1, blocking collectives, on_device(): outlook_records = lax.all_gather(mine, 'zone', axis=0, tiled=True)  31.8 us
    dot_general x3, matrix products, on_device(): jnp.einsum('shp,hsz->hpz', record_elements, adjoint, preferred_element_ty...  19.4 us
    psum x1, blocking collectives, on_device(): loss_sum, weight_total = lax.psum((sums, weight_part), ('zone', 'hour'))  17.4 us
    unnamed x78, local copies, waits for them, and re-layouts  14 us
    dot_general x3, matrix products, inside_climate_state(): jnp.einsum('shp,hpz->hsz', record_elements, coeff[initial_clock_time:init...  13.7 us
  transfers between devices with their start and end apart: 1, of which 0 were waited for; matrix products, arithmetic and copies ran while one was open for 1% of the time, Pallas kernels for 0%

profile of v1, /device:TPU:0, one launch (start us, length us, event | category | flops | bytes accessed | tf_op | source)
XLA Modules:
  0.0 231.8 jit_solution(18109823604304292025)
XLA Ops:
  0.7 1.1 slice_bitcast_fusion.1
  1.8 1.0 reshape.81
  2.8 3.4 %all-to-all-start = ((bf16[2,2,24576]{2,1,0:T(2,128)(2,1)}), bf16[2,2,24576]{2,1,0:T(2,128)(2,1)S(1)}, u32[]{:S(2)}, u32[]{:S(2)}) async-start(bf16[2,2,24576]{2,1,0:T(2,128)(2,1)} %reshape.81), calls=%async_computation | async-start | bytes 393216 | tf_op jit(solution)/shard_map/all_to_all | solution.py:42
  6.3 1.5 fusion.21
  8.1 31.8 %all_gather.16 = bf16[256,24,64]{2,1,0:T(8,128)(2,1)S(1)} all-gather(bf16[64,24,64]{2,1,0:T(8,128)(2,1)S(1)} %bitcast.22), channel_id=1, replica_groups=mesh['groups'=2,'zone'=4,'scen'=2,'hour'=2] {'zone'}, dimensions={0}, use_global_device_ids=true | all-gather | bytes 983040 | tf_op jit(solution)/shard_map/all_gather | solution.py:81
  40.0 1.2 fusion.29
  41.2 2.3 copy.18
  43.5 4.5 %gather_fusion = s32[1024]{0:T(1024)S(1)} fusion(s32[1024]{0:T(1024)S(1)} %copy-done.1, s32[1024]{0:T(1024)S(1)} %fusion.22), kind=kCustom, calls=%fused_computation | custom fusion | bytes 12288 | tf_op jit(solution)/shard_map/jit(_take)/gather | solution.py:34
  48.1 4.0 %gather_fusion.1 = f32[1024,64]{1,0:T(8,128)} fusion(f32[64,64]{1,0:T(8,128)S(1)} %copy-done, s32[1024]{0:T(1024)S(1)} %fusion.23), kind=kCustom, calls=%fused_computation.1 | custom fusion | bytes 528384 | tf_op jit(solution)/shard_map/jit(_take)/gather | solution.py:35
  52.1 2.1 select_bitcast_fusion
  54.2 1.2 copy.14
  56.7 2.0 copy.17
  58.8 2.0 copy.19
  61.4 1.5 fusion.30
  62.9 2.7 %multiply_convert_fusion.3 = bf16[24,64,1024]{2,1,0:T(8,128)(2,1)} fusion(bf16[24,64,1024]{2,1,0:T(8,128)(2,1)S(1)} %copy-done.2, f32[64,1024]{1,0:T(8,128)S(1)} %copy.14), kind=kLoop, calls=%fused_computation.21 | loop fusion | flops 4718592 | bytes 6553600 | tf_op jit(solution)/shard_map/convert_element_type | solution.py:36
  66.9 4.9 %fusion.5 = (u8[256,1024]{1,0:T(8,128)(4,1)S(1)}, u8[256,1024]{1,0:T(8,128)(4,1)S(1)}, f32[8,256,1024]{2,1,0:T(8,128)S(1)}) fusion(f32[8,1024]{1,0:T(8,128)} %get-tuple-element.36, f32[8,1024]{1,0:T(8,128)} %get-tuple-element.56, bf16[256,8,64]{0,2,1:T(8,128)(2,1)} %copy.18, bf16[24,64,1024]{2,1,0:T(8,128)(2,1)} %multiply_convert_fusion.3), kind=kOutput, calls=%fused_computation.30 | convolution fusion | flops 293076992 | bytes 10289152 | tf_op jit(solution)/shard_map/shp,hpz->hsz/dot_general | solution.py:50
  71.9 4.4 %fusion.3 = (u8[256,1024]{1,0:T(8,128)(4,1)S(1)}, u8[256,1024]{1,0:T(8,128)(4,1)S(1)}, f32[8,256,1024]{2,1,0:T(8,128)S(1)}) fusion(f32[8,1024]{1,0:T(8,128)S(1)} %copy-done.12, f32[8,1024]{1,0:T(8,128)S(1)} %copy-done.13, bf16[256,8,64]{0,2,1:T(8,128)(2,1)S(1)} %copy-done.7, bf16[24,64,1024]{2,1,0:T(8,128)(2,1)S(1)} %copy-done.3), kind=kOutput, calls=%fused_computation.28 | convolution fusion | flops 293076992 | bytes 10289152 | tf_op jit(solution)/shard_map/shp,hpz->hsz/dot_general | solution.py:50
  76.4 4.4 %fusion.7 = (u8[256,1024]{1,0:T(8,128)(4,1)S(1)}, u8[256,1024]{1,0:T(8,128)(4,1)S(1)}, f32[8,256,1024]{2,1,0:T(8,128)S(1)}) fusion(f32[8,1024]{1,0:T(8,128)S(1)} %copy-done.10, f32[8,1024]{1,0:T(8,128)S(1)} %copy-done.11, bf16[256,8,64]{0,2,1:T(8,128)(2,1)S(1)} %copy-done.5, bf16[24,64,1024]{2,1,0:T(8,128)(2,1)S(1)} %copy-done.3), kind=kOutput, calls=%fused_computation.32 | convolution fusion | flops 293076992 | bytes 10289152 | tf_op jit(solution)/shard_map/shp,hpz->hsz/dot_general | solution.py:50
  80.9 11.0 %multiply_reduce_fusion.1 = f32[256]{0:T(256)S(1)} fusion(f32[8,256,1024]{2,1,0:T(8,128)S(1)} %get-tuple-element.53, f32[8,1024]{1,0:T(8,128)S(1)} %copy-done.21, f32[8,1024]{1,0:T(8,128)S(1)} %copy-done.16, f32[8,1024]{1,0:T(8,128)S(1)} %copy-done.15, u8[256,1024]{1,0:T(8,128)(4,1)S(1)} %get-tuple-element.13, u8[256,1024]{1,0:T(8,128)(4,1)S(1)} %get-tuple-element.12), kind=kLoop, calls=%fused_computation.19 | loop fusion | flops 46137088 | bytes 9012224 | tf_op jit(solution)/shard_map/reduce_sum | solution.py:67
  91.9 10.8 %multiply_reduce_fusion.2 = f32[256]{0:T(256)S(1)} fusion(f32[8,256,1024]{2,1,0:T(8,128)S(1)} %get-tuple-element.52, f32[8,1024]{1,0:T(8,128)S(1)} %copy-done.19, f32[8,1024]{1,0:T(8,128)S(1)} %copy-done.13, f32[8,1024]{1,0:T(8,128)S(1)} %copy-done.12, u8[256,1024]{1,0:T(8,128)(4,1)S(1)} %get-tuple-element.20, u8[256,1024]{1,0:T(8,128)(4,1)S(1)} %get-tuple-element.14), kind=kLoop, calls=%fused_computation.20 | loop fusion | flops 46137088 | bytes 9012224 | tf_op jit(solution)/shard_map/reduce_sum | solution.py:67
  102.8 11.2 %multiply_reduce_fusion = f32[256]{0:T(256)S(1)} fusion(f32[8,256,1024]{2,1,0:T(8,128)S(1)} %get-tuple-element.51, f32[8,1024]{1,0:T(8,128)S(1)} %copy-done.17, f32[8,1024]{1,0:T(8,128)S(1)} %copy-done.11, f32[8,1024]{1,0:T(8,128)S(1)} %copy-done.10, u8[256,1024]{1,0:T(8,128)(4,1)S(1)} %get-tuple-element.22, u8[256,1024]{1,0:T(8,128)(4,1)S(1)} %get-tuple-element.21), kind=kLoop, calls=%fused_computation.18 | loop fusion | flops 46137088 | bytes 9012224 | tf_op jit(solution)/shard_map/reduce_sum | solution.py:67
  113.9 17.4 %all-reduce.3 = (f32[256]{0:T(256)S(1)}, f32[]{:T(128)}) all-reduce(f32[256]{0:T(256)S(1)} %add_add_fusion, f32[]{:T(128)S(6)} %mul.142), channel_id=1, replica_groups=mesh['groups'=2,'zone'=4,'scen'=2,'hour'=2] {'zone','hour'}, use_global_device_ids=true, to_apply=%region_3.4 | all-reduce | flops 257 | bytes 2056 | tf_op jit(solution)/shard_map/psum | solution.py:71
  131.3 1.2 fusion.28
  133.2 1.3 exponential_reduce_fusion
  134.5 1.4 dynamic-update-slice
  136.5 2.5 %dynamic-update-slice.1 = f32[2]{0:T(128)} dynamic-update-slice(f32[2]{0:T(128)} %broadcast.77.clone, f32[1]{0:T(128)} %bitcast.8, u32[]{:T(128)} %bitcast.5) | dynamic-update-slice | bytes 12
  139.0 5.0 %all-reduce.4 = (f32[2]{0:T(128)S(1)}, f32[2]{0:T(128)S(1)}) all-reduce(f32[2]{0:T(128)} %dynamic-update-slice.1, f32[2]{0:T(128)} %copy-done.26), channel_id=1, replica_groups=mesh['groups'=2,'zone'=4,'scen'=2,'hour'=2] {'scen'}, use_global_device_ids=true, to_apply=%add.1 | all-reduce | flops 4 | bytes 32
  150.0 8.2 %multiply_reduce_fusion.4 = f32[64,1024]{1,0:T(8,128)} fusion(bf16[256,8,64]{0,2,1:T(8,128)(2,1)S(1)} %copy-done.4, f32[8,256,1024]{2,1,0:T(8,128)} %copy-done.30, f32[256]{0:T(256)S(1)} %exponential_divide_fusion, f32[8,1024]{1,0:T(8,128)} %get-tuple-element.42, f32[8,1024]{1,0:T(8,128)} %get-tuple-element.56, f32[8,1024]{1,0:T(8,128)} %get-tuple-element.36, ...), kind=kOutput, calls=%fused_computation.26 | convolution fusion | flops 295108608 | bytes 10060800 | tf_op jit(solution)/shard_map/shp,hsz->hpz/dot_general | solution.py:93
  158.3 5.6 %multiply_reduce_fusion.5 = f32[64,1024]{1,0:T(8,128)} fusion(bf16[256,8,64]{0,2,1:T(8,128)(2,1)S(1)} %copy-done.8, f32[8,256,1024]{2,1,0:T(8,128)S(1)} %copy-done.29, f32[256]{0:T(256)S(1)} %exponential_divide_fusion, f32[8,1024]{1,0:T(8,128)S(1)} %copy-done.20, f32[8,1024]{1,0:T(8,128)S(1)} %copy-done.14, f32[8,1024]{1,0:T(8,128)S(1)} %copy-done.12, ...), kind=kOutput, calls=%fused_computation.27 | convolution fusion | flops 295108608 | bytes 10060800 | tf_op jit(solution)/shard_map/shp,hsz->hpz/dot_general | solution.py:93
  163.9 5.6 %multiply_reduce_fusion.3 = f32[64,1024]{1,0:T(8,128)} fusion(bf16[256,8,64]{0,2,1:T(8,128)(2,1)S(1)} %copy-done.6, f32[8,256,1024]{2,1,0:T(8,128)S(1)} %bitcast.24, f32[256]{0:T(256)S(1)} %exponential_divide_fusion, f32[8,1024]{1,0:T(8,128)S(1)} %copy-done.18, f32[8,1024]{1,0:T(8,128)S(1)} %copy-done.11, f32[8,1024]{1,0:T(8,128)S(1)} %copy-done.10, ...), kind=kOutput, calls=%fused_computation.25 | convolution fusion | flops 295108608 | bytes 10060800 | tf_op jit(solution)/shard_map/shp,hsz->hpz/dot_general | solution.py:93
  169.5 1.6 convolution_multiply_fusion
  171.2 57.6 %all-reduce.2 = f32[64,64]{1,0:T(8,128)S(1)} all-reduce(f32[64,64]{1,0:T(8,128)S(1)} %convolution_multiply_fusion), channel_id=2, replica_groups=mesh['groups'=2,'zone'=4,'scen'=2,'hour'=2] {'zone','scen','hour'}, use_global_device_ids=true, to_apply=%region_12.13.clone | all-reduce | flops 4096 | bytes 32768
  (86 shorter events, 6.0 us)
Async XLA Ops:
  0.6 47.5 %copy-start = (f32[64,64]{1,0:T(8,128)S(1)}, f32[64,64]{1,0:T(8,128)}, u32[]{:S(2)}) copy-start(f32[64,64]{1,0:T(8,128)} %param.9) | copy-start | bytes 49156
  0.6 42.9 %copy-start.23 = (s32[1024]{0:T(1024)S(1)}, s32[1024]{0:T(1024)}, u32[]{:S(2)}) copy-start(s32[1024]{0:T(1024)} %param.10) | copy-start | bytes 12292
  0.7 42.9 %copy-start.1 = (s32[1024]{0:T(1024)S(1)}, s32[1024]{0:T(1024)}, u32[]{:S(2)}) copy-start(s32[1024]{0:T(1024)} %param.11) | copy-start | bytes 12292
  2.8 5.0 %all-to-all-start = ((bf16[2,2,24576]{2,1,0:T(2,128)(2,1)}), bf16[2,2,24576]{2,1,0:T(2,128)(2,1)S(1)}, u32[]{:S(2)}, u32[]{:S(2)}) async-start(bf16[2,2,24576]{2,1,0:T(2,128)(2,1)} %reshape.81), calls=%async_computation | async-start | bytes 393216 | tf_op jit(solution)/shard_map/all_to_all | solution.py:42
  8.1 47.9 %copy-start.22 = (f32[1024]{0:T(1024)S(1)}, f32[1024]{0:T(1024)}, u32[]{:S(2)}) copy-start(f32[1024]{0:T(1024)} %param.13) | copy-start | bytes 12292
  40.0 22.9 %copy-start.2 = (bf16[24,64,1024]{2,1,0:T(8,128)(2,1)S(1)}, bf16[24,64,1024]{2,1,0:T(8,128)(2,1)}, u32[]{:S(2)}) copy-start(bf16[24,64,1024]{2,1,0:T(8,128)(2,1)} %param.8) | copy-start | bytes 9437188
  66.8 5.0 %copy-start.3 = (bf16[24,64,1024]{2,1,0:T(8,128)(2,1)S(1)}, bf16[24,64,1024]{2,1,0:T(8,128)(2,1)}, u32[]{:S(2)}) copy-start(bf16[24,64,1024]{2,1,0:T(8,128)(2,1)} %multiply_convert_fusion.3) | copy-start | bytes 9437188
  66.9 5.0 %copy-start.7 = (bf16[256,8,64]{0,2,1:T(8,128)(2,1)S(1)}, bf16[256,8,64]{0,2,1:T(8,128)(2,1)}, u32[]{:S(2)}) copy-start(bf16[256,8,64]{0,2,1:T(8,128)(2,1)} %copy.17) | copy-start | bytes 786436
  66.9 5.0 %copy-start.12 = (f32[8,1024]{1,0:T(8,128)S(1)}, f32[8,1024]{1,0:T(8,128)}, u32[]{:S(2)}) copy-start(f32[8,1024]{1,0:T(8,128)} %get-tuple-element.38) | copy-start | bytes 98308
  66.9 5.0 %copy-start.13 = (f32[8,1024]{1,0:T(8,128)S(1)}, f32[8,1024]{1,0:T(8,128)}, u32[]{:S(2)}) copy-start(f32[8,1024]{1,0:T(8,128)} %get-tuple-element.54) | copy-start | bytes 98308
  71.8 9.0 %copy-start.30 = (f32[8,256,1024]{2,1,0:T(8,128)}, f32[8,256,1024]{2,1,0:T(8,128)S(1)}, u32[]{:S(2)}) copy-start(f32[8,256,1024]{2,1,0:T(8,128)S(1)} %get-tuple-element.53) | copy-start | bytes 25165828
  71.9 4.5 %copy-start.5 = (bf16[256,8,64]{0,2,1:T(8,128)(2,1)S(1)}, bf16[256,8,64]{0,2,1:T(8,128)(2,1)}, u32[]{:S(2)}) copy-start(bf16[256,8,64]{0,2,1:T(8,128)(2,1)} %copy.19) | copy-start | bytes 786436
  71.9 4.5 %copy-start.10 = (f32[8,1024]{1,0:T(8,128)S(1)}, f32[8,1024]{1,0:T(8,128)}, u32[]{:S(2)}) copy-start(f32[8,1024]{1,0:T(8,128)} %get-tuple-element.37) | copy-start | bytes 98308
  76.3 15.6 %copy-start.28 = (f32[8,256,1024]{2,1,0:T(8,128)}, f32[8,256,1024]{2,1,0:T(8,128)S(1)}, u32[]{:S(2)}) copy-start(f32[8,256,1024]{2,1,0:T(8,128)S(1)} %get-tuple-element.52) | copy-start | bytes 25165828
  76.3 4.5 %copy-start.15 = (f32[8,1024]{1,0:T(8,128)S(1)}, f32[8,1024]{1,0:T(8,128)}, u32[]{:S(2)}) copy-start(f32[8,1024]{1,0:T(8,128)} %get-tuple-element.36) | copy-start | bytes 98308
  76.4 4.5 %copy-start.16 = (f32[8,1024]{1,0:T(8,128)S(1)}, f32[8,1024]{1,0:T(8,128)}, u32[]{:S(2)}) copy-start(f32[8,1024]{1,0:T(8,128)} %get-tuple-element.56) | copy-start | bytes 98308
  76.4 4.5 %copy-start.21 = (f32[8,1024]{1,0:T(8,128)S(1)}, f32[8,1024]{1,0:T(8,128)}, u32[]{:S(2)}) copy-start(f32[8,1024]{1,0:T(8,128)} %get-tuple-element.42) | copy-start | bytes 98308
  80.8 22.0 %copy-start.27 = (f32[8,256,1024]{2,1,0:T(8,128)}, f32[8,256,1024]{2,1,0:T(8,128)S(1)}, u32[]{:S(2)}) copy-start(f32[8,256,1024]{2,1,0:T(8,128)S(1)} %get-tuple-element.51) | copy-start | bytes 25165828
  80.8 11.1 %copy-start.19 = (f32[8,1024]{1,0:T(8,128)S(1)}, f32[8,1024]{1,0:T(8,128)}, u32[]{:S(2)}) copy-start(f32[8,1024]{1,0:T(8,128)} %get-tuple-element.44) | copy-start | bytes 98308
  91.9 10.9 %copy-start.17 = (f32[8,1024]{1,0:T(8,128)S(1)}, f32[8,1024]{1,0:T(8,128)}, u32[]{:S(2)}) copy-start(f32[8,1024]{1,0:T(8,128)} %get-tuple-element.43) | copy-start | bytes 98308
  102.7 29.9 %copy-start.25 = (u32[32]{0:T(128)S(1)}, u32[32]{0:T(128)}, u32[]{:S(2)}) copy-start(u32[32]{0:T(128)} %constant.81) | copy-start | bytes 388
  102.7 47.2 %copy-start.4 = (bf16[256,8,64]{0,2,1:T(8,128)(2,1)S(1)}, bf16[256,8,64]{0,2,1:T(8,128)(2,1)}, u32[]{:S(2)}) copy-start(bf16[256,8,64]{0,2,1:T(8,128)(2,1)} %copy.18) | copy-start | bytes 786436
  150.0 8.3 %copy-start.8 = (bf16[256,8,64]{0,2,1:T(8,128)(2,1)S(1)}, bf16[256,8,64]{0,2,1:T(8,128)(2,1)}, u32[]{:S(2)}) copy-start(bf16[256,8,64]{0,2,1:T(8,128)(2,1)} %copy.17) | copy-start | bytes 786436
  150.0 8.2 %copy-start.14 = (f32[8,1024]{1,0:T(8,128)S(1)}, f32[8,1024]{1,0:T(8,128)}, u32[]{:S(2)}) copy-start(f32[8,1024]{1,0:T(8,128)} %get-tuple-element.54) | copy-start | bytes 98308
  150.0 8.2 %copy-start.20 = (f32[8,1024]{1,0:T(8,128)S(1)}, f32[8,1024]{1,0:T(8,128)}, u32[]{:S(2)}) copy-start(f32[8,1024]{1,0:T(8,128)} %get-tuple-element.44) | copy-start | bytes 98308
  150.0 8.2 %copy-start.29 = (f32[8,256,1024]{2,1,0:T(8,128)S(1)}, f32[8,256,1024]{2,1,0:T(8,128)}, u32[]{:S(2)}) copy-start(f32[8,256,1024]{2,1,0:T(8,128)} %copy-done.28) | copy-start | bytes 25165828
  150.0 13.9 %slice-start = ((s8[8388608]{0:T(1024)(128)(4,1)}), s8[4194304]{0:T(1024)(128)(4,1)S(1)}, s32[]{:S(2)}) async-start(s8[8388608]{0:T(1024)(128)(4,1)} %bitcast.23), calls=%async_computation.1 | async-start | bytes 8388608
  158.2 5.7 %copy-start.6 = (bf16[256,8,64]{0,2,1:T(8,128)(2,1)S(1)}, bf16[256,8,64]{0,2,1:T(8,128)(2,1)}, u32[]{:S(2)}) copy-start(bf16[256,8,64]{0,2,1:T(8,128)(2,1)} %copy.19) | copy-start | bytes 786436
  158.3 5.6 %copy-start.18 = (f32[8,1024]{1,0:T(8,128)S(1)}, f32[8,1024]{1,0:T(8,128)}, u32[]{:S(2)}) copy-start(f32[8,1024]{1,0:T(8,128)} %get-tuple-element.43) | copy-start | bytes 98308
  158.3 5.6 %slice-start.1 = ((s8[8388608]{0:T(1024)(128)(4,1)}), s8[4194304]{0:T(1024)(128)(4,1)S(1)}, s32[]{:S(2)}) async-start(s8[8388608]{0:T(1024)(128)(4,1)} %bitcast.23), calls=%async_computation.2 | async-start | bytes 8388608
  163.9 5.6 %copy-start.9 = (f32[64,1024]{1,0:T(8,128)S(1)}, f32[64,1024]{1,0:T(8,128)}, u32[]{:S(2)}) copy-start(f32[64,1024]{1,0:T(8,128)} %multiply_reduce_fusion.4) | copy-start | bytes 786436
  163.9 64.9 %copy-start.24 = (u32[32]{0:T(128)S(1)}, u32[32]{0:T(128)}, u32[]{:S(2)}) copy-start(u32[32]{0:T(128)} %constant.93) | copy-start | bytes 388
  (2 other events, 5.0 us)
